TPU v7x, 32 devices: a whole 2x2x4 slice. The times are simulated.
32 devices in a mesh: dp: 4 (over y, x), ctx: 8 (over z, core).
Axes of the slice: x: 2, y: 2, z: 4, core: 2. Of those that a mesh axis runs over, the one named last changes fastest.
Arguments:
- inputs: bfloat16 [8192, 8192], P(('dp', 'ctx')), parts along dimension 0, may hold values from -6 to 6
- key_query: bfloat16 [8192, 2048], P(('dp', 'ctx')), parts along dimension 0, may hold values from -3 to 3
- conv_inputs: float32 [4, 8192], replicated, may hold values from -3 to 3
- conv_kq: float32 [4, 2048], replicated, may hold values from -3 to 3
- step_size: float32 [8192, 128], P(('dp', 'ctx')), parts along dimension 0, may hold values from 0.1 to 1
- decay_log: float32 [8192, 128], P(('dp', 'ctx')), parts along dimension 0, may hold values from -1 to 0, as said below
- skip_gain: float32 [128], replicated, may hold values from 0.5 to 1.5
- norm_gain: float32 [8192], replicated, may hold values from 0.5 to 1.5
Outputs:
- mixed: bfloat16 [8192, 8192], P('dp', 'ctx'), parts along dimension 0
There are 4 independent parts, one for each index of `dp`. A program takes and returns all parts, laid end to end along the dimension named above; an argument that names none is the same for every part. Nothing has to cross between parts.
Inputs may be any that keep to these rules, and one draw needn't show every extreme that they name: `decay_log`: log decay factors, all negative.
All inputs are finite; a program needn't handle non-finite values.
Results may differ from a plain program's by a relative error of at most 0.0085.
Values may be sent and summed in bfloat16 or wider, within the bound.
No kernel may reach another device: no remote copies, remote signals or barrier semaphores. Data moves between devices by JAX's collectives and lax.ppermute only.
A program may use at most 448 MiB of HBM per device.

v0:
```python
import jax
import jax.numpy as jnp
from jax import lax
from jax.sharding import PartitionSpec as P

HEADS = 128
HEAD_DIM = 64
STATE = 128
GROUPS = 8
KW = 4
BLOCK = 128
TOK_DEV = 256


def passed_along(x, axis, by):
    peers = lax.axis_size(axis)
    pairs = [(i, i + by) for i in range(peers) if 0 <= i + by < peers]
    return lax.ppermute(x, axis, pairs)


def carried_in(part, axis, combine, identity):
    place = lax.axis_index(axis)
    gathered = jax.tree.map(lambda a: lax.all_gather(a, axis), part)
    state = jax.tree.map(lambda a, e: jnp.zeros_like(a) + jnp.asarray(e, a.dtype), part, identity)

    def one(hop, state):
        return combine(
            state, jax.tree.map(lambda a: lax.dynamic_index_in_dim(a, hop, 0, False), gathered)
        )

    return lax.fori_loop(0, place, one, state)


def convolve(values, rim, weight):
    length = values.shape[0]
    padded = jnp.concatenate([rim, values], axis=0).astype(jnp.float32)
    summed = jnp.zeros(values.shape, jnp.float32)
    for offset in range(KW):
        summed = summed + weight[offset][None, :] * padded[offset : offset + length]
    return jax.nn.silu(summed).astype(jnp.bfloat16)


def block_terms(scaled, b_part, c_part, decays):
    groups = scaled.shape[1]
    per_group = scaled.shape[2]
    cumul = jnp.cumsum(decays, axis=0)
    upper = cumul.T
    slot_numbers = lax.broadcasted_iota(jnp.int32, (BLOCK, BLOCK), 0)
    sources = lax.broadcasted_iota(jnp.int32, (BLOCK, BLOCK), 1)
    spread = jnp.where(
        (slot_numbers >= sources)[None], upper[:, :, None] - upper[:, None, :], -jnp.inf
    )
    decay_mat = jnp.exp(spread).reshape(groups, per_group, BLOCK, BLOCK)
    scores = jnp.einsum("tgn,sgn->gts", c_part, b_part, preferred_element_type=jnp.float32)
    weights = (scores[:, None] * decay_mat).astype(jnp.bfloat16)
    intra = jnp.einsum("ghts,sghp->tghp", weights, scaled, preferred_element_type=jnp.float32)
    last = cumul[-1]
    fade = jnp.exp(last[None, :] - cumul).reshape(BLOCK, groups, per_group)
    keyed = (b_part[:, :, None, :].astype(jnp.float32) * fade[:, :, :, None]).astype(jnp.bfloat16)
    state = jnp.einsum("sghn,sghp->ghnp", keyed, scaled, preferred_element_type=jnp.float32)
    return (intra, state.reshape(groups * per_group, STATE, HEAD_DIM), last, cumul)


def carried(c_part, incoming, cumul):
    groups = c_part.shape[1]
    per_group = incoming.shape[0] // groups
    held = incoming.astype(jnp.bfloat16).reshape(groups, per_group, STATE, HEAD_DIM)
    term = jnp.einsum("tgn,ghnp->tghp", c_part, held, preferred_element_type=jnp.float32)
    return term * jnp.exp(cumul).reshape(BLOCK, groups, per_group)[:, :, :, None]


def finish(intra, inter, x_block, skip_gain, norm_gain):
    per_group = HEADS // GROUPS
    skipped = skip_gain.reshape(GROUPS, per_group)[None, :, :, None] * x_block.reshape(
        BLOCK, GROUPS, per_group, HEAD_DIM
    ).astype(jnp.float32)
    summed = (intra + inter + skipped).reshape(BLOCK, GROUPS, per_group * HEAD_DIM)
    power = jnp.mean(summed * summed, axis=-1, keepdims=True)
    normed = (
        summed * lax.rsqrt(power + 1e-05) * norm_gain.reshape(GROUPS, per_group * HEAD_DIM)[None]
    )
    return normed.reshape(BLOCK, HEADS * HEAD_DIM).astype(jnp.bfloat16)


def chain(earlier, later):
    return (earlier[0] + later[0], jnp.exp(later[0])[..., None, None] * earlier[1] + later[1])


def by_positions(
    inputs, key_query, conv_inputs, conv_kq, step_size, decay_log, skip_gain, norm_gain
):
    per_group = HEADS // GROUPS
    width = GROUPS * STATE
    channels = HEADS * HEAD_DIM
    tail = TOK_DEV - KW + 1
    rims = passed_along(jnp.concatenate([inputs[tail:], key_query[tail:]], axis=1), "ctx", 1)
    x_conv = convolve(inputs, rims[:, :channels], conv_inputs)
    kq_conv = convolve(key_query, rims[:, channels:], conv_kq)
    scaled = (
        x_conv.reshape(TOK_DEV, HEADS, HEAD_DIM).astype(jnp.float32) * step_size[:, :, None]
    ).astype(jnp.bfloat16)
    count = TOK_DEV // BLOCK
    x_blocks = x_conv.reshape(count, BLOCK, channels)
    s_blocks = scaled.reshape(count, BLOCK, GROUPS, per_group, HEAD_DIM)
    b_blocks = kq_conv[:, :width].reshape(count, BLOCK, GROUPS, STATE)
    c_blocks = kq_conv[:, width:].reshape(count, BLOCK, GROUPS, STATE)
    d_blocks = decay_log.reshape(count, BLOCK, HEADS)
    intra_all, states, lasts, cumuls = lax.map(
        lambda piece: block_terms(*piece), (s_blocks, b_blocks, c_blocks, d_blocks)
    )

    def local_step(carry, piece):
        total_log, held = carry
        last, state = piece
        return ((total_log + last, jnp.exp(last)[:, None, None] * held + state), (total_log, held))

    start = (jnp.zeros((HEADS,), jnp.float32), jnp.zeros((HEADS, STATE, HEAD_DIM), jnp.float32))
    (dev_log, dev_state), (before_log, local_in) = lax.scan(local_step, start, (lasts, states))
    identity = (jnp.zeros_like(dev_log), jnp.zeros_like(dev_state))
    prefix = carried_in((dev_log, dev_state), "ctx", chain, identity)
    incoming = prefix[1]
    block_in = jnp.exp(before_log)[:, :, None, None] * incoming[None] + local_in

    def produce(piece):
        c_block, carry, cumul, intra, x_block = piece
        return finish(intra, carried(c_block, carry, cumul), x_block, skip_gain, norm_gain)

    normed = lax.map(produce, (c_blocks, block_in, cumuls, intra_all, x_blocks)).reshape(
        TOK_DEV, channels
    )
    return lax.all_to_all(normed, "ctx", split_axis=1, concat_axis=0, tiled=True)


def per_device(inputs, key_query, conv_inputs, conv_kq, step_size, decay_log, skip_gain, norm_gain):
    return by_positions(
        inputs, key_query, conv_inputs, conv_kq, step_size, decay_log, skip_gain, norm_gain
    )


def solution(mesh):
    in_specs = (
        P(("dp", "ctx"), None),
        P(("dp", "ctx"), None),
        P(),
        P(),
        P(("dp", "ctx"), None),
        P(("dp", "ctx"), None),
        P(),
        P(),
    )
    out_specs = P("dp", "ctx")
    return jax.shard_map(
        per_device, mesh=mesh, in_specs=in_specs, out_specs=out_specs, check_vma=False
    )
```

profile of v0, /device:TPU:12, one launch (start us, length us, event | category | flops | bytes accessed | tf_op | source)
XLA Modules:
  0.0 762.4 jit_solution(3555533044496442740)
XLA Ops:
  6.5 0.9 slice.70
  7.5 0.8 slice.71
  8.3 1.9 collective-permute-start
  10.2 1.4 fusion.41
  11.6 0.9 fusion.42
  12.6 1.0 copy.49
  14.1 1.5 maximum_convert_fusion.1
  15.6 1.3 multiply_convert_fusion.8
  17.2 1.9 copy-done.6
  19.1 1.2 maximum_convert_fusion
  20.3 6.5 multiply_convert_fusion.7
  26.8 7.0 copy.48
  33.9 10.8 %reshape.160 = f32[2,128,8,16,64]{1,0,4,3,2:T(2,128)} reshape(f32[256,8192]{0,1:T(8,128)} %copy.48) | data formatting | bytes 16777216 | tf_op jit(solution)/shard_map/convert_element_type | solution.py:100
  44.7 10.1 %multiply_convert_fusion.6 = bf16[2,128,8,16,64]{1,0,4,3,2:T(2,128)(2,1)} fusion(f32[2,128,8,16,64]{1,0,4,3,2:T(2,128)} %reshape.160, f32[2,128,8,16]{1,0,3,2:T(2,128)S(1)} %mul.222), kind=kLoop, calls=%fused_computation.68 | loop fusion | flops 4194304 | bytes 12713984 | tf_op jit(solution)/shard_map/convert_element_type | solution.py:101
  54.8 5.3 copy.51
  60.2 31.4 %while.55 = (s32[]{:T(128)}, f32[2,128,8,16,64]{1,4,3,2,0:T(8,128)}, f32[2,128,128,64]{2,3,1,0:T(8,128)}, f32[2,128]{1,0:T(2,128)S(1)}, f32[2,128,128]{2,1,0:T(8...) while((s32[]{:T(128)}, ...), condition=%wide.region_2.3_spmd, body=%wide.region_0.2_spmd.sunk | while | flops 585252864 | bytes 92509896 | solution.py:108
  60.8 5.2 fusion.60
  66.9 2.9 copy-done.2
  70.0 5.8 bitcast_dynamic-update-slice_fusion.8
  76.5 5.2 fusion.60
  82.7 2.9 copy-done.2
  85.7 5.8 bitcast_dynamic-update-slice_fusion.8
  91.6 0.8 copy-done.4
  92.4 49.7 %while.58 = (s32[]{:T(128)}, f32[128]{0:T(128)S(1)}, f32[128,128,64]{2,1,0:T(8,128)}, f32[2,128]{1,0:T(2,128)S(1)}, f32[2,128,128,64]{3,2,1,0:T(8,128)}, /*index...) while((s32[]{:T(128)}, f32[128]{0:T(128)S(1)}, ...), condition=%wide.region_4.5_spmd.clone, body=%wide.region_3.4_spmd.clone.sunk | while | flops 4194563 | bytes 79696528 | solution.py:118
  92.4 5.3 bitcast_dynamic-update-slice_fusion.11
  97.7 2.3 constant_dynamic-slice_fusion.15
  100.1 6.9 copy.95
  107.0 7.5 bitcast_add_fusion.5
  114.5 8.4 %bitcast_dynamic-update-slice_fusion.11 = f32[2,128,128,64]{3,2,1,0:T(8,128)} fusion(f32[2,128,128,64]{3,2,1,0:T(8,128)} %get-tuple-element.650, s32[]{:T(128)} %get-tuple-element.646, f32[128,128,64]{2,1,0:T(8,128)} %get-tuple-element.648, pred[]{:T(512)S(6)} %compare.3), kind=kLoop, calls=%fused_computation.19.clone.1 | loop fusion | flops 1048576 | bytes 16777728 | tf_op jit(solution)/shard_map/while/body/jit(dynamic_update_index_in_dim)/dynamic_update_slice | solution.py:108
  122.9 2.3 constant_dynamic-slice_fusion.15
  125.2 6.9 copy.95
  132.1 9.9 %bitcast_add_fusion.5 = f32[128,128,64]{2,1,0:T(8,128)} fusion(f32[1,128,128,64]{3,2,1,0:T(8,128)} %copy.95, f32[128,128,64]{2,1,0:T(8,128)} %get-tuple-element.648, f32[128]{0:T(128)S(1)} %get-tuple-element.599, pred[]{:T(512)S(6)} %compare.3), kind=kLoop, calls=%fused_computation.20.clone.1 | loop fusion | flops 3145728 | bytes 12583425 | tf_op jit(solution)/shard_map/while/body/eval_jaxpr/add | solution.py:115
  142.1 6.8 copy.55
  148.9 9.0 %all-gather.2 = f32[8,1,128]{2,1,0:T(1,128)S(1)} all-gather(f32[1,1,128]{2,1,0:T(1,128)S(1)} %bitcast.176), channel_id=2, replica_groups=mesh['dp'=4,'ctx'=8] {'ctx'}, dimensions={0}, use_global_device_ids=true | all-gather | bytes 4608 | tf_op jit(solution)/shard_map/all_gather | solution.py:23
  157.9 278.1 %all-gather.5.cloned.1.call-done = f32[1024,128,64]{1,2,0:T(8,128)} async-done(((f32[128,128,64]{1,2,0:T(8,128)}), f32[1024,128,64]{1,2,0:T(8,128)}) %all-gather.5.cloned.1.call-update) | async-done | bytes 33554448 | tf_op jit(solution)/shard_map/all_gather | solution.py:23
  436.0 4.3 broadcast.75
  440.3 43.1 %while.56 = (s32[]{:T(128)}, f32[128,128,64]{2,1,0:T(8,128)}, s32[]{:T(128)}, f32[8,128]{1,0:T(8,128)S(1)}, f32[8,128,128,64]{2,3,1,0:T(8,128)}, /*index=5*/s32[]{:T(128)}, s32[]{:T(128)}, s32[]{:T(128)}) while((s32[]{:T(128)}, f32[128,128,64]{2,1,0:T(8,128)}, s32[]{:T(128)}, f32[8,128]{1,0:T(8,128)S(1)}, f32[8,128,128,64]{2,3,1,0:T(8,128)}, ...), condition=%wide.region_6.7_spmd, body=%wide.region_5.6_spmd.sunk | while | flops 2097157 | bytes 29361792 | solution.py:31
  440.3 4.8 constant_dynamic-slice_fusion.12
  445.1 6.9 copy.91
  451.9 9.9 %bitcast_add_fusion.4 = f32[128,128,64]{2,1,0:T(8,128)} fusion(f32[1,128,128,64]{3,2,1,0:T(8,128)} %copy.91, f32[128,128,64]{2,1,0:T(8,128)} %get-tuple-element.673, f32[128]{0:T(128)S(1)} %exponential_bitcast_fusion.2), kind=kLoop, calls=%fused_computation.clone.1 | loop fusion | flops 2097152 | bytes 12583424 | tf_op jit(solution)/shard_map/while/body/add | solution.py:86
  461.8 4.8 constant_dynamic-slice_fusion.12
  466.6 6.9 copy.91
  473.5 9.9 %bitcast_add_fusion.4 = f32[128,128,64]{2,1,0:T(8,128)} fusion(f32[1,128,128,64]{3,2,1,0:T(8,128)} %copy.91, f32[128,128,64]{2,1,0:T(8,128)} %get-tuple-element.673, f32[128]{0:T(128)S(1)} %exponential_bitcast_fusion.2), kind=kLoop, calls=%fused_computation.clone.1 | loop fusion | flops 2097152 | bytes 12583424 | tf_op jit(solution)/shard_map/while/body/add | solution.py:86
  483.4 12.0 %multiply_add_fusion = bf16[2,128,128,64]{3,2,1,0:T(8,128)(2,1)} fusion(f32[2,128,128,64]{3,2,1,0:T(8,128)} %get-tuple-element.193, f32[128,128,64]{2,1,0:T(8,128)} %get-tuple-element.192, f32[2,128]{1,0:T(2,128)S(1)} %exp.52), kind=kLoop, calls=%fused_computation.60 | loop fusion | flops 6291456 | bytes 16778240 | tf_op jit(solution)/shard_map/add | solution.py:122
  495.4 8.6 %copy.57 = bf16[2,128,128,64]{2,3,1,0:T(8,128)(2,1)} copy(bf16[2,128,128,64]{3,2,1,0:T(8,128)(2,1)} %multiply_add_fusion) | data formatting | bytes 8388608 | tf_op jit(solution)/shard_map/while | solution.py:128
  504.1 36.6 %while.57 = (s32[]{:T(128)}, bf16[2,128,8192]{2,1,0:T(8,128)(2,1)}, f32[2,128,8,16,64]{1,4,3,2,0:T(8,128)}, bf16[2,128,128,64]{2,3,1,0:T(8,128)(2,1)}, bf16[2,12...) while((s32[]{:T(128)}, bf16[2,128,8192]{2,1,0:T(8,128)(2,1)}, ...), condition=%wide.region_9.10_spmd, body=%wide.region_7.9_spmd.sunk | while | flops 278922240 | bytes 49011340 | solution.py:128
  504.1 1.7 constant_dynamic-slice_fusion.13
  505.8 2.5 copy.92
  508.3 3.3 dynamic-slice_convert_fusion.2
  511.8 4.0 multiply_reduce_fusion.2
  515.7 2.2 fusion.62
  518.0 2.9 copy.94
  520.9 1.5 constant_dynamic-update-slice_fusion.2
  522.4 1.7 constant_dynamic-slice_fusion.13
  524.1 2.5 copy.92
  526.6 3.3 dynamic-slice_convert_fusion.2
  530.0 4.0 multiply_reduce_fusion.2
  534.0 2.2 fusion.62
  536.3 2.9 copy.94
  539.2 1.5 constant_dynamic-update-slice_fusion.2
  540.6 6.5 copy.73
  547.1 2.3 copy.62
  549.5 204.0 %all_to_all.19 = bf16[256,8,1024]{2,0,1:T(8,128)(2,1)S(1)} all-to-all(bf16[256,8,1024]{2,0,1:T(8,128)(2,1)S(1)} %copy.62), channel_id=1, replica_groups=mesh['dp'=4,'ctx'=8] {'ctx'}, dimensions={1} | all-to-all | bytes 8388608 | tf_op jit(solution)/shard_map/all_to_all | solution.py:131
  753.5 2.0 copy.149
  (93 shorter events, 4.7 us)
Async XLA Ops:
  6.5 429.5 %all-gather.5.cloned.1.call-start = ((), (), s32[]{:S(2)}) async-start(), calls=%async_computation.1 | async-start | bytes 37748736 | tf_op jit(solution)/shard_map/all_gather | solution.py:23
  8.3 5.8 collective-permute-start
  16.9 2.2 copy-start.6
  54.7 5.4 copy-start.8
  60.8 5.2 copy-start.1
  66.6 3.3 copy-start.2
  76.5 5.2 copy-start.1
  82.3 3.3 copy-start.2
  91.6 0.8 copy-start.4
  91.6 0.8 copy-start.9
  92.4 5.3 copy-start.3
  114.5 8.4 %copy-start.3 = (f32[2,128,128,64]{2,3,1,0:T(8,128)S(1)}, f32[2,128,128,64]{2,3,1,0:T(8,128)}, u32[]{:S(2)}) copy-start(f32[2,128,128,64]{2,3,1,0:T(8,128)} %get-tuple-element.661) | copy-start | bytes 25165828 | tf_op jit(solution)/shard_map/while
  495.4 8.7 %copy-start.5 = (bf16[2,128,8,128]{3,1,2,0:T(8,128)(2,1)S(1)}, bf16[2,128,8,128]{3,1,2,0:T(8,128)(2,1)}, u32[]{:S(2)}) copy-start(bf16[2,128,8,128]{3,1,2,0:T(8,128)(2,1)} %copy-done.4) | copy-start | bytes 1572868
  495.4 8.7 %copy-start.7 = (f32[8192]{0:T(1024)S(1)}, f32[8192]{0:T(1024)}, u32[]{:S(2)}) copy-start(f32[8192]{0:T(1024)} %param.23) | copy-start | bytes 98308
  495.4 8.7 %copy-start.10 = (f32[2,128,128]{2,1,0:T(8,128)S(1)}, f32[2,128,128]{2,1,0:T(8,128)}, u32[]{:S(2)}) copy-start(f32[2,128,128]{2,1,0:T(8,128)} %copy-done.9) | copy-start | bytes 393220
  495.4 8.7 %copy-start.11 = (f32[128]{0:T(128)S(1)}, f32[128]{0:T(128)}, u32[]{:S(2)}) copy-start(f32[128]{0:T(128)} %param.22) | copy-start | bytes 1540
  508.3 3.5 copy-start
  526.6 3.5 copy-start
Sparse Core Ops, SparseCore 0:
  149.0 286.9 all-gather.4
where the time goes:
time: 768 us; the launch traced here: 762 us
  waiting for transfers between devices  279 us (36%)
  blocking collectives  213 us (28%)
  local copies, waits for them, and re-layouts  136 us (18%)
  other arithmetic  88.8 us (12%)
  matrix products  30.6 us (4%)
  between operations  13.7 us (2%)
    all_gather x1, waiting for transfers between devices, carried_in(): gathered = jax.tree.map(lambda a: lax.all_gather(a, axis), part)  278 us
    all_to_all x1, blocking collectives, by_positions(): lax.all_to_all(normed, 'ctx', split_axis=1, concat_axis=0, tiled=True)  204 us
    dynamic_slice x4, local copies, waits for them, and re-layouts, one(): lax.dynamic_index_in_dim(a, hop, 0, False)  23.3 us
    add x2, other arithmetic, chain(): jnp.exp(later[0])[..., None, None] * earlier[1] + later[1]  19.8 us
    dynamic_slice x4, local copies, waits for them, and re-layouts, by_positions(): lax.scan(local_step, start, (lasts, states))  18.5 us
    convert_element_type x2, local copies, waits for them, and re-layouts, by_positions(): x_conv.reshape(TOK_DEV, HEADS, HEAD_DIM).astype(jnp.float32)  17.8 us
    add x2, other arithmetic, local_step(): jnp.exp(last)[:, None, None] * held + state  17.4 us
  transfers between devices with their start and end apart: 2, of which 2 were waited for; matrix products, arithmetic and copies ran while one was open for 0% of the time, Pallas kernels for 0%

commit v1 on v0

v1 whole, which is shorter than its diff:
```python
import functools

import jax
import jax.numpy as jnp
from jax import lax
from jax.experimental import pallas as pl
from jax.experimental.pallas import tpu as pltpu
from jax.sharding import PartitionSpec as P

HEADS = 128
HEAD_DIM = 64
STATE = 128
GROUPS = 8
KW = 4
BLOCK = 128
GROUP_WIDTH = HEADS * HEAD_DIM // GROUPS
EPS = 1e-05
HALO = 8
TILE = 256


def contract(a, b, dims):
    return lax.dot_general(a, b, (dims, ((), ())), preferred_element_type=jnp.float32)


def contract_exact(a, b, dims):
    return lax.dot_general(
        a,
        b,
        (dims, ((), ())),
        preferred_element_type=jnp.float32,
        precision=lax.Precision.HIGHEST,
    )


def mixer_kernel(peers, whole_group, *refs):
    me_ref = refs[0]
    parts = refs[1 : 1 + peers]
    auxes = refs[1 + peers : 1 + 2 * peers]
    taps_ref, skip_ref, gain_ref = refs[1 + 2 * peers : 4 + 2 * peers]
    outs = refs[4 + 2 * peers : 5 + 2 * peers + (0 if whole_group else 1)]
    raw, aux, wide, carry, total_ref, sems = refs[-6:]
    step = pl.program_id(0)
    me = me_ref[0]
    rows = raw.shape[1]
    width = outs[0].shape[1]
    heads = width // HEAD_DIM

    @pl.when(step == 0)
    def _():
        for k in range(peers):
            source = lax.rem(me + (peers - k), peers)
            pltpu.make_async_copy(parts[k], raw.at[source], sems.at[0, source]).start()
            pltpu.make_async_copy(auxes[k], aux.at[source], sems.at[1, source]).start()
        carry[...] = jnp.zeros_like(carry)
        wide[rows : rows + HALO] = jnp.zeros((HALO, wide.shape[1]), jnp.float32)

    pltpu.make_async_copy(parts[0], raw.at[step], sems.at[0, step]).wait()
    pltpu.make_async_copy(auxes[0], aux.at[step], sems.at[1, step]).wait()

    wide[0:HALO] = wide[rows : rows + HALO]
    wide[HALO : HALO + rows] = raw[step].astype(jnp.float32)

    row = lax.broadcasted_iota(jnp.int32, (BLOCK, BLOCK), 0)
    col = lax.broadcasted_iota(jnp.int32, (BLOCK, BLOCK), 1)
    lower = row >= col
    tril = jnp.where(lower, 1.0, 0.0).astype(jnp.float32)
    eye = jnp.where(row == col, 1.0, 0.0).astype(jnp.float32)
    head_of = lax.broadcasted_iota(jnp.int32, (2 * heads, width), 1) // HEAD_DIM
    head_row = lax.rem(lax.broadcasted_iota(jnp.int32, (2 * heads, width), 0), heads)
    spread = jnp.where(head_of == head_row, 1.0, 0.0).astype(jnp.bfloat16)

    def halves(v):
        high = v.astype(jnp.bfloat16)
        low = (v - high.astype(jnp.float32)).astype(jnp.bfloat16)
        return jnp.concatenate([high, low], axis=1)

    def activated(start, lo, hi):
        summed = taps_ref[0:1, lo:hi] * wide[pl.ds(start, BLOCK), lo:hi]
        for k in range(1, KW):
            summed = summed + taps_ref[k : k + 1, lo:hi] * wide[pl.ds(start + k, BLOCK), lo:hi]
        return (summed / (1.0 + jnp.exp(-summed))).astype(jnp.bfloat16)

    for block in range(rows // BLOCK):
        top = block * BLOCK
        start = top + HALO - KW + 1
        decays = aux[step, 0:heads, top : top + BLOCK]
        steps = aux[step, heads : 2 * heads, top : top + BLOCK]
        cumul = contract_exact(tril, decays, ((1,), (1,)))
        steps = contract_exact(eye, steps, ((1,), (1,)))
        middle = cumul[BLOCK // 2 - 1 : BLOCK // 2]
        inward = halves(steps * jnp.exp(middle - cumul))
        outward = halves(
            jnp.concatenate(
                [jnp.exp(cumul - middle), jnp.broadcast_to(jnp.exp(middle), (16, heads))], axis=0
            )
        )
        b_part = activated(start, width, width + STATE)
        c_part = activated(start, width + STATE, width + 2 * STATE)
        scores = contract(c_part, b_part, ((1,), (1,)))
        scores = jnp.where(lower, scores, 0.0).astype(jnp.bfloat16)
        left = jnp.concatenate([scores, c_part], axis=1)
        power = jnp.zeros((BLOCK, 1), jnp.float32)
        for lo in range(0, width, TILE):
            hi = lo + TILE
            x_conv = activated(start, lo, hi).astype(jnp.float32)
            scaled = (x_conv * contract(inward, spread[:, lo:hi], ((1,), (0,)))).astype(
                jnp.bfloat16
            )
            out_scale = contract(outward, spread[:, lo:hi], ((1,), (0,)))
            held = carry[:, lo:hi] * out_scale[BLOCK : BLOCK + 1]
            right = jnp.concatenate([scaled, held.astype(jnp.bfloat16)], axis=0)
            mixed = contract(left, right, ((1,), (0,)))
            total = mixed * out_scale[:BLOCK] + skip_ref[0:1, lo:hi] * x_conv
            total_ref[:, lo:hi] = total
            power = power + jnp.sum(total * total, axis=1, keepdims=True)
            added = contract(b_part, scaled, ((0,), (0,)))
            carry[:, lo:hi] = (held + added) * out_scale[BLOCK - 1 : BLOCK]
        if whole_group:
            norm = lax.rsqrt(power * (1.0 / GROUP_WIDTH) + EPS)
            for lo in range(0, width, TILE):
                hi = lo + TILE
                outs[0][top : top + BLOCK, lo:hi] = (
                    total_ref[:, lo:hi] * norm * gain_ref[0:1, lo:hi]
                ).astype(jnp.bfloat16)
        else:
            outs[0][top : top + BLOCK, :] = total_ref[...]
            outs[1][top : top + BLOCK, :] = jnp.broadcast_to(power, (BLOCK, 128))


def per_device(inputs, key_query, conv_inputs, conv_kq, step_size, decay_log, skip_gain, norm_gain):
    peers = lax.axis_size("ctx")
    me = lax.axis_index("ctx")
    rows = inputs.shape[0]
    width = HEADS * HEAD_DIM // peers
    heads = HEADS // peers
    span = GROUP_WIDTH // width
    scalars = jnp.concatenate(
        [
            decay_log.T.reshape(peers, heads, rows),
            step_size.T.reshape(peers, heads, rows),
        ],
        axis=1,
    )

    def columns(a, first, size):
        return lax.dynamic_slice_in_dim(a, first, size, axis=1)

    def message(x, kq, owner):
        group = owner // span
        return jnp.concatenate(
            [
                columns(x, owner * width, width),
                columns(kq, group * STATE, STATE),
                columns(kq, (GROUPS + group) * STATE, STATE),
            ],
            axis=1,
        )

    parts = []
    auxes = []
    for k in range(peers):
        owner = lax.rem(me + k, peers)
        part = message(inputs, key_query, owner)
        scalar = lax.dynamic_index_in_dim(scalars, owner, 0, False)
        if k:
            pairs = [(i, (i + k) % peers) for i in range(peers)]
            part = lax.ppermute(part, "ctx", pairs)
            scalar = lax.ppermute(scalar, "ctx", pairs)
        parts.append(part)
        auxes.append(scalar)

    taps = message(conv_inputs, conv_kq, me)
    skip = columns(jnp.repeat(skip_gain, HEAD_DIM)[None], me * width, width)
    gain = columns(norm_gain[None], me * width, width)

    whole_group = span == 1
    total_rows = peers * rows
    out_shape = [
        jax.ShapeDtypeStruct((total_rows, width), jnp.bfloat16 if whole_group else jnp.float32)
    ]
    out_specs = [pl.BlockSpec((rows, width), lambda i: (i, 0))]
    if not whole_group:
        out_shape.append(jax.ShapeDtypeStruct((total_rows, 128), jnp.float32))
        out_specs.append(pl.BlockSpec((rows, 128), lambda i: (i, 0)))
    any_spec = pl.BlockSpec(memory_space=pl.ANY)
    full = width + 2 * STATE
    outs = pl.pallas_call(
        functools.partial(mixer_kernel, peers, whole_group),
        grid=(peers,),
        in_specs=[pl.BlockSpec(memory_space=pltpu.SMEM)]
        + [any_spec] * (2 * peers)
        + [
            pl.BlockSpec((KW, full), lambda i: (0, 0)),
            pl.BlockSpec((1, width), lambda i: (0, 0)),
            pl.BlockSpec((1, width), lambda i: (0, 0)),
        ],
        out_specs=out_specs,
        out_shape=out_shape,
        scratch_shapes=[
            pltpu.VMEM((peers, rows, full), jnp.bfloat16),
            pltpu.VMEM((peers, 2 * heads, rows), jnp.float32),
            pltpu.VMEM((rows + HALO, full), jnp.float32),
            pltpu.VMEM((STATE, width), jnp.float32),
            pltpu.VMEM((BLOCK, width), jnp.float32),
            pltpu.SemaphoreType.DMA((2, peers)),
        ],
        compiler_params=pltpu.CompilerParams(vmem_limit_bytes=40 * 1024 * 1024),
        cost_estimate=pl.CostEstimate(
            flops=2 * total_rows * width * 450,
            bytes_accessed=total_rows * (2 * full + 2 * width),
            transcendentals=total_rows * full,
        ),
        name="mixer",
    )(me.reshape(1).astype(jnp.int32), *parts, *auxes, taps, skip, gain)
    if whole_group:
        return outs[0]
    total, power = outs
    sharers = [list(range(i, i + span)) for i in range(0, peers, span)]
    power = lax.psum(power[:, :1], "ctx", axis_index_groups=sharers)
    return (total * lax.rsqrt(power * (1.0 / GROUP_WIDTH) + EPS) * gain).astype(jnp.bfloat16)


def solution(mesh):
    in_specs = (
        P(("dp", "ctx"), None),
        P(("dp", "ctx"), None),
        P(),
        P(),
        P(("dp", "ctx"), None),
        P(("dp", "ctx"), None),
        P(),
        P(),
    )
    out_specs = P("dp", "ctx")
    return jax.shard_map(
        per_device, mesh=mesh, in_specs=in_specs, out_specs=out_specs, check_vma=False
    )
```

time: 768 us -> 162 us (0.21)
  the two profiles are of different devices: /device:TPU:12 before, /device:TPU:11 now
where the time goes in v1:
time: 162 us
  starting transfers between devices  66.5 us (41%)
  waiting for transfers between devices  51.9 us (32%)
  Pallas kernels  27.8 us (17%)
  local copies, waits for them, and re-layouts  8.73 us (5%)
  other arithmetic  6.77 us (4%)
    ppermute x7, starting transfers between devices, per_device(): part = lax.ppermute(part, 'ctx', pairs)  57.4 us
    ppermute x7, waiting for transfers between devices, per_device(): part = lax.ppermute(part, 'ctx', pairs)  38.6 us
    pallas_call x1, Pallas kernels, per_device(): pl.pallas_call(functools.partial(mixer_kernel, peers, whole_group), grid=...  27.8 us
    ppermute x7, waiting for transfers between devices, per_device(): scalar = lax.ppermute(scalar, 'ctx', pairs)  13.3 us
    ppermute x7, starting transfers between devices, per_device(): scalar = lax.ppermute(scalar, 'ctx', pairs)  9.12 us
    concatenate x9, other arithmetic, message(): jnp.concatenate([columns(x, owner * width, width), columns(kq, group * ST...  5.5 us
    dynamic_slice x5, local copies, waits for them, and re-layouts, columns(): return lax.dynamic_slice_in_dim(a, first, size, axis=1)  5.22 us
  transfers between devices with their start and end apart: 14, of which 4 were waited for; matrix products, arithmetic and copies ran while one was open for 8% of the time, Pallas kernels for 0%

profile of v1, /device:TPU:11, one launch (start us, length us, event | category | flops | bytes accessed | tf_op | source)
XLA Modules:
  0.0 161.8 jit_solution(16747351225304604734)
XLA Ops:
  0.0 0.0 copy-start
  0.0 1.0 copy.12
  1.0 1.0 copy.11
  2.1 0.6 fusion.15
  2.7 0.2 collective-permute-start.12
  2.8 4.2 %collective-permute-start.11 = (f32[32,256]{1,0:T(8,128)}, f32[32,256]{1,0:T(8,128)S(1)}, u32[]{:S(2)}, u32[]{:S(2)}) collective-permute-start(f32[32,256]{1,0:T(8,128)} %get-tuple-element.36), channel_id=1, source_target_pairs={{0,5},{1,6},{2,7},{3,0},{4,1},{5,2},{6,3},{7,4},{8,13},{9,14},{10,... | collective-permute-start | bytes 98312 | tf_op jit(solution)/shard_map/ppermute | solution.py:169
  7.0 0.7 fusion.1
  7.7 0.0 collective-permute-start.13
  7.7 0.0 copy-start.1
  7.7 2.8 %constant_dynamic-slice_fusion.6 = (bf16[256,1024]{1,0:T(8,128)(2,1)S(1)}, bf16[256,1024]{1,0:T(8,128)(2,1)S(1)}, bf16[256,1024]{1,0:T(8,128)(2,1)S(1)}, bf16[25...) fusion(bf16[256,8192]{1,0:T(8,128)(2,1)} %param.8, ...), kind=kLoop, calls=%fused_computation.47 | loop fusion | bytes 8388640 | tf_op jit(solution)/shard_map/dynamic_slice | solution.py:147
  10.5 0.0 copy-done.1
  10.5 1.0 constant_dynamic-slice_fusion.5
  11.5 0.9 pad_maximum_fusion.6
  12.4 0.2 collective-permute-start.5
  12.6 0.9 pad_maximum_fusion.1
  13.5 2.0 %collective-permute-start = (bf16[256,1280]{1,0:T(8,128)(2,1)}, bf16[256,1280]{1,0:T(8,128)(2,1)S(1)}, u32[]{:S(2)}, u32[]{:S(2)}) collective-permute-start(bf16[256,1280]{1,0:T(8,128)(2,1)} %pad_maximum_fusion.1), channel_id=1, source_target_pairs={{0,1},{1,2},{2,3},{3,4},{4,5},{5,6},{6,7},{7,0},{8,9},{9,10},{10,1... | collective-permute-start | bytes 1966088 | tf_op jit(solution)/shard_map/ppermute | solution.py:168
  15.5 0.1 pad_maximum_fusion.7
  15.5 0.1 pad_maximum_fusion.5
  15.6 0.9 pad_maximum_fusion.4
  16.5 0.0 copy-start.2
  16.5 0.9 pad_maximum_fusion.3
  17.4 0.0 collective-permute-done.12.refs_15_
  17.4 0.0 collective-permute-start.7
  17.4 0.9 pad_maximum_fusion.2
  18.3 0.0 copy-done.2
  18.3 0.1 broadcast_in_dim.4
  18.4 0.7 broadcast_in_dim_reshape.3
  19.1 0.0 collective-permute-done.11.refs_14_
  19.1 1.3 collective-permute-start.8
  20.4 0.0 collective-permute-done.13.refs_16_
  20.4 1.6 %collective-permute-start.9 = (f32[32,256]{1,0:T(8,128)}, f32[32,256]{1,0:T(8,128)S(1)}, u32[]{:S(2)}, u32[]{:S(2)}) collective-permute-start(f32[32,256]{1,0:T(8,128)} %get-tuple-element.33), channel_id=1, source_target_pairs={{0,3},{1,4},{2,5},{3,6},{4,7},{5,0},{6,1},{7,2},{8,11},{9,12},{10,... | collective-permute-start | bytes 98312 | tf_op jit(solution)/shard_map/ppermute | solution.py:169
  22.0 13.3 %collective-permute-done.7.refs_10_ = f32[32,256]{1,0:T(8,128)S(1)} collective-permute-done((f32[32,256]{1,0:T(8,128)S(1)}, f32[32,256]{1,0:T(8,128)S(1)}, u32[]{:S(2)}, u32[]{:S(2)}) %collective-permute-start.7) | collective-permute-done | bytes 32800 | tf_op jit(solution)/shard_map/ppermute | solution.py:169
  35.3 1.9 %collective-permute-start.10 = (f32[32,256]{1,0:T(8,128)}, f32[32,256]{1,0:T(8,128)S(1)}, u32[]{:S(2)}, u32[]{:S(2)}) collective-permute-start(f32[32,256]{1,0:T(8,128)} %get-tuple-element.34), channel_id=1, source_target_pairs={{0,4},{1,5},{2,6},{3,7},{4,0},{5,1},{6,2},{7,3},{8,12},{9,13},{10,... | collective-permute-start | bytes 98312 | tf_op jit(solution)/shard_map/ppermute | solution.py:169
  37.2 0.7 constant_dynamic-slice_fusion.refs_18_
  37.8 0.7 dynamic-slice.3
  38.5 0.0 collective-permute-done.8.refs_11_
  38.5 0.0 collective-permute-start.1
  38.5 0.0 collective-permute-done.9.refs_12_
  38.5 4.6 %collective-permute-start.2 = (bf16[256,1280]{1,0:T(8,128)(2,1)}, bf16[256,1280]{1,0:T(8,128)(2,1)S(1)}, u32[]{:S(2)}, u32[]{:S(2)}) collective-permute-start(bf16[256,1280]{1,0:T(8,128)(2,1)} %pad_maximum_fusion.3), channel_id=1, source_target_pairs={{0,3},{1,4},{2,5},{3,6},{4,7},{5,0},{6,1},{7,2},{8,11},{9,12},{10,... | collective-permute-start | bytes 1966088 | tf_op jit(solution)/shard_map/ppermute | solution.py:168
  43.1 0.0 collective-permute-done.10.refs_13_
  43.1 1.7 %collective-permute-start.3 = (bf16[256,1280]{1,0:T(8,128)(2,1)}, bf16[256,1280]{1,0:T(8,128)(2,1)S(1)}, u32[]{:S(2)}, u32[]{:S(2)}) collective-permute-start(bf16[256,1280]{1,0:T(8,128)(2,1)} %pad_maximum_fusion.4), channel_id=1, source_target_pairs={{0,4},{1,5},{2,6},{3,7},{4,0},{5,1},{6,2},{7,3},{8,12},{9,13},{10,... | collective-permute-start | bytes 1966088 | tf_op jit(solution)/shard_map/ppermute | solution.py:168
  44.8 0.0 collective-permute-done.5.refs_7_
  44.8 48.9 %collective-permute-start.4 = (bf16[256,1280]{1,0:T(8,128)(2,1)S(1)}, bf16[256,1280]{1,0:T(8,128)(2,1)S(1)}, u32[]{:S(2)}, u32[]{:S(2)}) collective-permute-start(bf16[256,1280]{1,0:T(8,128)(2,1)S(1)} %pad_maximum_fusion.5), channel_id=1, source_target_pairs={{0,5},{1,6},{2,7},{3,0},{4,1},{5,2},{6,3},{7,4},{8,13},{9,14},{10,... | collective-permute-start | bytes 1966088 | tf_op jit(solution)/shard_map/ppermute | solution.py:168
  93.7 0.0 collective-permute-done.refs_2_
  93.7 0.0 collective-permute-start.6
  93.7 0.7 constant_dynamic-slice_fusion.2
  94.4 0.0 copy-done
  94.5 0.9 pad_maximum_fusion.refs_1_
  95.4 0.0 collective-permute-done.1.refs_3_
  95.4 0.0 collective-permute-done.2.refs_4_
  95.4 25.3 %collective-permute-done.3.refs_5_ = bf16[256,1280]{1,0:T(8,128)(2,1)S(1)} collective-permute-done((bf16[256,1280]{1,0:T(8,128)(2,1)}, bf16[256,1280]{1,0:T(8,128)(2,1)S(1)}, u32[]{:S(2)}, u32[]{:S(2)}) %collective-permute-start.3) | collective-permute-done | bytes 655392 | tf_op jit(solution)/shard_map/ppermute | solution.py:168
  120.7 5.5 %collective-permute-done.4.refs_6_ = bf16[256,1280]{1,0:T(8,128)(2,1)S(1)} collective-permute-done((bf16[256,1280]{1,0:T(8,128)(2,1)S(1)}, bf16[256,1280]{1,0:T(8,128)(2,1)S(1)}, u32[]{:S(2)}, u32[]{:S(2)}) %collective-permute-start.4) | collective-permute-done | bytes 655392 | tf_op jit(solution)/shard_map/ppermute | solution.py:168
  126.2 7.8 %collective-permute-done.6.refs_8_ = bf16[256,1280]{1,0:T(8,128)(2,1)S(1)} collective-permute-done((bf16[256,1280]{1,0:T(8,128)(2,1)S(1)}, bf16[256,1280]{1,0:T(8,128)(2,1)S(1)}, u32[]{:S(2)}, u32[]{:S(2)}) %collective-permute-start.6) | collective-permute-done | bytes 655392 | tf_op jit(solution)/shard_map/ppermute | solution.py:168
  134.0 27.8 %mixer.1 = bf16[2048,1024]{1,0:T(8,128)(2,1)} custom-call(s32[1]{0:T(128)} %bitcast.refs_0_, bf16[256,1280]{1,0:T(8,128)(2,1)S(1)} %pad_maximum_fusion.refs_1_, bf16[256,1280]{1,0:T(8,128)(2,1)S(1)} %collective-permute-done.refs_2_, bf16[256,1280]{1,0:T(8,128)(2,1)S(1)} %collective-permute-done.1.refs_3_, ...), custom_call_target="tpu_custom_call" | custom-call | flops 1887436800 | bytes 9437184 | tf_op jit(solution)/shard_map/mixer/pallas_call | solution.py:188
  (2 shorter events, 0.0 us)
Async XLA Ops:
  0.0 94.4 %copy-start = (f32[4,8192]{1,0:T(4,128)S(1)}, f32[4,8192]{1,0:T(4,128)}, u32[]{:S(2)}) copy-start(f32[4,8192]{1,0:T(4,128)} %param.10) | copy-start | bytes 393220
  2.7 14.7 %collective-permute-start.12 = (f32[32,256]{1,0:T(8,128)S(1)}, f32[32,256]{1,0:T(8,128)S(1)}, u32[]{:S(2)}, u32[]{:S(2)}) collective-permute-start(f32[32,256]{1,0:T(8,128)S(1)} %get-tuple-element.35), channel_id=1, source_target_pairs={{0,6},{1,7},{2,0},{3,1},{4,2},{5,3},{6,4},{7,5},{8,14},{9,15},{10,... | collective-permute-start | bytes 98312 | tf_op jit(solution)/shard_map/ppermute | solution.py:169
  2.8 16.2 %collective-permute-start.11 = (f32[32,256]{1,0:T(8,128)}, f32[32,256]{1,0:T(8,128)S(1)}, u32[]{:S(2)}, u32[]{:S(2)}) collective-permute-start(f32[32,256]{1,0:T(8,128)} %get-tuple-element.36), channel_id=1, source_target_pairs={{0,5},{1,6},{2,7},{3,0},{4,1},{5,2},{6,3},{7,4},{8,13},{9,14},{10,... | collective-permute-start | bytes 98312 | tf_op jit(solution)/shard_map/ppermute | solution.py:169
  7.7 12.7 %collective-permute-start.13 = (f32[32,256]{1,0:T(8,128)}, f32[32,256]{1,0:T(8,128)S(1)}, u32[]{:S(2)}, u32[]{:S(2)}) collective-permute-start(f32[32,256]{1,0:T(8,128)} %get-tuple-element.29), channel_id=1, source_target_pairs={{0,7},{1,0},{2,1},{3,2},{4,3},{5,4},{6,5},{7,6},{8,15},{9,8},{10,9... | collective-permute-start | bytes 98312 | tf_op jit(solution)/shard_map/ppermute | solution.py:169
  7.7 2.9 %copy-start.1 = (bf16[256,2048]{1,0:T(8,128)(2,1)S(1)}, bf16[256,2048]{1,0:T(8,128)(2,1)}, u32[]{:S(2)}) copy-start(bf16[256,2048]{1,0:T(8,128)(2,1)} %param.9) | copy-start | bytes 3145732
  12.4 32.4 %collective-permute-start.5 = (bf16[256,1280]{1,0:T(8,128)(2,1)}, bf16[256,1280]{1,0:T(8,128)(2,1)S(1)}, u32[]{:S(2)}, u32[]{:S(2)}) collective-permute-start(bf16[256,1280]{1,0:T(8,128)(2,1)} %pad_maximum_fusion.6), channel_id=1, source_target_pairs={{0,6},{1,7},{2,0},{3,1},{4,2},{5,3},{6,4},{7,5},{8,14},{9,15},{10,... | collective-permute-start | bytes 1966088 | tf_op jit(solution)/shard_map/ppermute | solution.py:168
  13.5 80.3 %collective-permute-start = (bf16[256,1280]{1,0:T(8,128)(2,1)}, bf16[256,1280]{1,0:T(8,128)(2,1)S(1)}, u32[]{:S(2)}, u32[]{:S(2)}) collective-permute-start(bf16[256,1280]{1,0:T(8,128)(2,1)} %pad_maximum_fusion.1), channel_id=1, source_target_pairs={{0,1},{1,2},{2,3},{3,4},{4,5},{5,6},{6,7},{7,0},{8,9},{9,10},{10,1... | collective-permute-start | bytes 1966088 | tf_op jit(solution)/shard_map/ppermute | solution.py:168
  16.5 1.8 %copy-start.2 = (f32[128]{0:T(128)S(1)}, f32[128]{0:T(128)}, u32[]{:S(2)}) copy-start(f32[128]{0:T(128)} %param.14) | copy-start | bytes 1540
  17.4 17.9 %collective-permute-start.7 = (f32[32,256]{1,0:T(8,128)S(1)}, f32[32,256]{1,0:T(8,128)S(1)}, u32[]{:S(2)}, u32[]{:S(2)}) collective-permute-start(f32[32,256]{1,0:T(8,128)S(1)} %get-tuple-element.31), channel_id=1, source_target_pairs={{0,1},{1,2},{2,3},{3,4},{4,5},{5,6},{6,7},{7,0},{8,9},{9,10},{10,1... | collective-permute-start | bytes 98312 | tf_op jit(solution)/shard_map/ppermute | solution.py:169
  19.1 19.4 %collective-permute-start.8 = (f32[32,256]{1,0:T(8,128)}, f32[32,256]{1,0:T(8,128)S(1)}, u32[]{:S(2)}, u32[]{:S(2)}) collective-permute-start(f32[32,256]{1,0:T(8,128)} %get-tuple-element.32), channel_id=1, source_target_pairs={{0,2},{1,3},{2,4},{3,5},{4,6},{5,7},{6,0},{7,1},{8,10},{9,11},{10,... | collective-permute-start | bytes 98312 | tf_op jit(solution)/shard_map/ppermute | solution.py:169
  20.4 18.1 %collective-permute-start.9 = (f32[32,256]{1,0:T(8,128)}, f32[32,256]{1,0:T(8,128)S(1)}, u32[]{:S(2)}, u32[]{:S(2)}) collective-permute-start(f32[32,256]{1,0:T(8,128)} %get-tuple-element.33), channel_id=1, source_target_pairs={{0,3},{1,4},{2,5},{3,6},{4,7},{5,0},{6,1},{7,2},{8,11},{9,12},{10,... | collective-permute-start | bytes 98312 | tf_op jit(solution)/shard_map/ppermute | solution.py:169
  35.3 7.8 %collective-permute-start.10 = (f32[32,256]{1,0:T(8,128)}, f32[32,256]{1,0:T(8,128)S(1)}, u32[]{:S(2)}, u32[]{:S(2)}) collective-permute-start(f32[32,256]{1,0:T(8,128)} %get-tuple-element.34), channel_id=1, source_target_pairs={{0,4},{1,5},{2,6},{3,7},{4,0},{5,1},{6,2},{7,3},{8,12},{9,13},{10,... | collective-permute-start | bytes 98312 | tf_op jit(solution)/shard_map/ppermute | solution.py:169
  38.5 56.9 %collective-permute-start.1 = (bf16[256,1280]{1,0:T(8,128)(2,1)}, bf16[256,1280]{1,0:T(8,128)(2,1)S(1)}, u32[]{:S(2)}, u32[]{:S(2)}) collective-permute-start(bf16[256,1280]{1,0:T(8,128)(2,1)} %pad_maximum_fusion.2), channel_id=1, source_target_pairs={{0,2},{1,3},{2,4},{3,5},{4,6},{5,7},{6,0},{7,1},{8,10},{9,11},{10,... | collective-permute-start | bytes 1966088 | tf_op jit(solution)/shard_map/ppermute | solution.py:168
  38.5 56.9 %collective-permute-start.2 = (bf16[256,1280]{1,0:T(8,128)(2,1)}, bf16[256,1280]{1,0:T(8,128)(2,1)S(1)}, u32[]{:S(2)}, u32[]{:S(2)}) collective-permute-start(bf16[256,1280]{1,0:T(8,128)(2,1)} %pad_maximum_fusion.3), channel_id=1, source_target_pairs={{0,3},{1,4},{2,5},{3,6},{4,7},{5,0},{6,1},{7,2},{8,11},{9,12},{10,... | collective-permute-start | bytes 1966088 | tf_op jit(solution)/shard_map/ppermute | solution.py:168
  43.1 77.6 %collective-permute-start.3 = (bf16[256,1280]{1,0:T(8,128)(2,1)}, bf16[256,1280]{1,0:T(8,128)(2,1)S(1)}, u32[]{:S(2)}, u32[]{:S(2)}) collective-permute-start(bf16[256,1280]{1,0:T(8,128)(2,1)} %pad_maximum_fusion.4), channel_id=1, source_target_pairs={{0,4},{1,5},{2,6},{3,7},{4,0},{5,1},{6,2},{7,3},{8,12},{9,13},{10,... | collective-permute-start | bytes 1966088 | tf_op jit(solution)/shard_map/ppermute | solution.py:168
  44.8 81.4 %collective-permute-start.4 = (bf16[256,1280]{1,0:T(8,128)(2,1)S(1)}, bf16[256,1280]{1,0:T(8,128)(2,1)S(1)}, u32[]{:S(2)}, u32[]{:S(2)}) collective-permute-start(bf16[256,1280]{1,0:T(8,128)(2,1)S(1)} %pad_maximum_fusion.5), channel_id=1, source_target_pairs={{0,5},{1,6},{2,7},{3,0},{4,1},{5,2},{6,3},{7,4},{8,13},{9,14},{10,... | collective-permute-start | bytes 1966088 | tf_op jit(solution)/shard_map/ppermute | solution.py:168
  93.7 40.3 %collective-permute-start.6 = (bf16[256,1280]{1,0:T(8,128)(2,1)S(1)}, bf16[256,1280]{1,0:T(8,128)(2,1)S(1)}, u32[]{:S(2)}, u32[]{:S(2)}) collective-permute-start(bf16[256,1280]{1,0:T(8,128)(2,1)S(1)} %pad_maximum_fusion.7), channel_id=1, source_target_pairs={{0,7},{1,0},{2,1},{3,2},{4,3},{5,4},{6,5},{7,6},{8,15},{9,8},{10,9... | collective-permute-start | bytes 1966088 | tf_op jit(solution)/shard_map/ppermute | solution.py:168
